TPU v7x, 32 devices: a whole 2x2x4 slice. The times are simulated.
32 devices in a mesh: groups: 2 (over y), blk: 4 (over z), draw: 2 (over x), sub: 2 (over core).
Axes of the slice: x: 2, y: 2, z: 4, core: 2. Of those that a mesh axis runs over, the one named last changes fastest.
Arguments:
- white_noise: float32 [4, 32, 128, 128], P(None, ('groups', 'blk', 'sub'), 'draw'), parts along dimension 1, may hold values from -6 to 6
- coupling: bfloat16 [4, 32, 6, 128, 128], P(None, ('groups', 'blk', 'sub')), parts along dimension 1, may hold values from -0.21875 to 0.21875
- diag_inv: bfloat16 [4, 32, 128, 128], P(None, ('groups', 'blk', 'sub')), parts along dimension 1, may hold values from -0.5 to 0.5
- prior_far: bfloat16 [32, 128, 128], P(('groups', 'blk', 'sub'), 'draw'), parts along dimension 0, may hold values from -6 to 6
- prior_near: bfloat16 [32, 128, 128], P(('groups', 'blk', 'sub'), 'draw'), parts along dimension 0, may hold values from -6 to 6
- neighbours: int32 [4, 32, 6], P(None, ('groups', 'blk', 'sub')), parts along dimension 1, may hold values from 0 to 15, as said below
- spot_map: int32 [16384], P(('groups', 'blk', 'sub')), parts along dimension 0, may hold values from 0 to 8191, as said below
Outputs:
- posterior_draws: bfloat16 [128, 16384], P('draw', ('groups', 'blk', 'sub')), parts along dimension 1
There are 2 independent parts, one for each index of `groups`. A program takes and returns all parts, laid end to end along the dimension named above; each array names one. Nothing has to cross between parts.
Inputs may be any that keep to these rules, and one draw needn't show every extreme that they name: Entries index blocks of one level; an owner holds the aligned runs of 2 blocks of each level. For every owner of reading blocks, every level of solved blocks and every owner of those blocks, at most 2 distinct blocks of that owner are read by the reading owner's blocks of the two levels that read that level, and this most is reached in every draw; the neighbours of one block are distinct. `spot_map`: A permutation of 0 .. 8191. Every aligned run of 1024 entries (one owner's points) places exactly 128 points in every spatial shard, a shard being an aligned run of 1024 positions.
All inputs are finite; a program needn't handle non-finite values.
Results may differ from a plain program's by a relative error of at most 0.0063.
Values may be sent and summed in bfloat16 or wider, within the bound.
A program may use at most 64 MiB of HBM per device.

v0:
```python
import jax
import jax.numpy as jnp
from jax import lax
from jax.sharding import PartitionSpec as P

K1 = 4
LEVELS = 4


def lookup(gathered, neighbour_ids):
    return jnp.take(gathered, neighbour_ids, axis=0)


def shards(white_noise, coupling, diag_inv, prior_far, prior_near, neighbours, spot_map):
    owners = lax.axis_size(("blk", "sub"))
    draw_count = white_noise.shape[2]
    point_count = spot_map.shape[0]
    per_pair = point_count // owners

    def share_section(solved):
        gathered = lax.all_gather(solved, ("blk", "sub"), axis=0, tiled=True)
        return (gathered, None)

    section_pools = [share_section(prior_far), share_section(prior_near)]
    levels = []
    for level_idx in range(LEVELS):
        neighbour_ids = neighbours[level_idx]
        older_pool, older_table = section_pools[level_idx]
        newer_pool, newer_table = section_pools[level_idx + 1]
        older_rows = lookup(older_pool, neighbour_ids[:, K1:])
        carried_old = jnp.einsum(
            "bkfp,bkpq->bfq",
            older_rows,
            coupling[level_idx][:, K1:],
            preferred_element_type=jnp.float32,
        )
        fresh_rows = lookup(newer_pool, neighbour_ids[:, :K1])
        carried_new = jnp.einsum(
            "bkfp,bkpq->bfq",
            fresh_rows,
            coupling[level_idx][:, :K1],
            preferred_element_type=jnp.float32,
        )
        remain = (white_noise[level_idx] - carried_old - carried_new).astype(jnp.bfloat16)
        solved = jnp.einsum(
            "bfp,bpq->bfq", remain, diag_inv[level_idx], preferred_element_type=jnp.float32
        ).astype(jnp.bfloat16)
        levels.append(solved)
        if level_idx + 2 <= LEVELS:
            section_pools.append(share_section(solved))
    ordering = jnp.argsort(spot_map)
    sorted_spots = jnp.take(spot_map, ordering).reshape(owners, per_pair)
    placings = lax.all_to_all(sorted_spots, ("blk", "sub"), split_axis=0, concat_axis=0, tiled=True)
    stacked = jnp.stack(levels)
    local_draws = stacked.transpose(2, 0, 1, 3).reshape(draw_count, point_count)
    moving = jnp.take(local_draws, ordering, axis=1).reshape(draw_count, owners, per_pair)
    arrived = lax.all_to_all(moving, ("blk", "sub"), split_axis=1, concat_axis=1, tiled=True)
    spot_local = placings.reshape(-1) % point_count
    result = jnp.zeros((draw_count, point_count), jnp.bfloat16)
    return result.at[:, spot_local].set(arrived.reshape(draw_count, point_count))


def solution(mesh):
    return jax.shard_map(
        shards,
        mesh=mesh,
        in_specs=(
            P(None, ("groups", "blk", "sub"), "draw", None),
            P(None, ("groups", "blk", "sub"), None, None, None),
            P(None, ("groups", "blk", "sub"), None, None),
            P(("groups", "blk", "sub"), "draw", None),
            P(("groups", "blk", "sub"), "draw", None),
            P(None, ("groups", "blk", "sub"), None),
            P(("groups", "blk", "sub")),
        ),
        out_specs=P("draw", ("groups", "blk", "sub")),
        check_vma=False,
    )
```

profile of v0, /device:TPU:0, one launch (start us, length us, event | category | flops | bytes accessed | tf_op | source)
XLA Modules:
  0.0 119.0 jit_solution(10001052654322083775)
XLA Ops:
  0.0 5.1 %sort.17 = (s32[1024]{0:T(1024)}, s32[1024]{0:T(1024)S(1)}) sort(s32[1024]{0:T(1024)} %param.17, s32[1024]{0:T(1024)S(1)} %iota.4), dimensions={0}, to_apply=%region_0.1 | sort | flops 10240 | bytes 16384 | tf_op jit(solution)/shard_map/jit(argsort)/sort | solution.py:51
  5.1 0.0 copy-done
  5.1 0.0 copy-start.6
  5.1 0.0 copy-start.4
  5.2 0.0 copy-start.5
  5.2 0.0 copy-start.1
  5.2 4.5 %gather_fusion = s32[1024]{0:T(1024)S(1)} fusion(s32[1024]{0:T(1024)S(1)} %copy-done, s32[1024]{0:T(1024)S(1)} %fusion.80), kind=kCustom, calls=%fused_computation.8 | custom fusion | bytes 12288 | tf_op jit(solution)/shard_map/jit(_take)/gather | solution.py:52
  9.7 0.6 broadcast_select_fusion.1
  10.3 6.3 %all-to-all-start = ((s32[8,1,128]{2,1,0:T(1,128)}), s32[8,1,128]{2,1,0:T(1,128)S(1)}, u32[]{:S(2)}, u32[]{:S(2)}) async-start(s32[8,1,128]{2,1,0:T(1,128)} %bitcast), calls=%async_computation | async-start | bytes 8192 | tf_op jit(solution)/shard_map/all_to_all | solution.py:53
  16.6 0.0 copy-done.6
  16.7 0.1 compare_and_fusion.2
  16.8 0.1 compare_and_fusion.6
  16.8 0.1 compare_and_fusion.8
  16.9 0.1 compare_and_fusion.4
  17.0 0.1 compare_select_fusion.5
  17.1 0.1 compare_select_fusion.9
  17.2 0.1 compare_select_fusion.11
  17.2 0.1 compare_select_fusion.7
  17.3 0.1 reshape.255
  17.4 0.1 reshape.251
  17.5 0.1 reshape.239
  17.6 0.1 reshape.235
  17.6 0.1 reshape.231
  17.7 0.1 reshape.227
  17.8 0.1 reshape.247
  17.9 0.1 reshape.243
  18.1 0.0 copy-done.4
  18.1 14.7 %all_gather.16 = bf16[16,64,128]{2,1,0:T(8,128)(2,1)S(1)} all-gather(bf16[2,64,128]{2,1,0:T(8,128)(2,1)S(1)} %copy-done.4), channel_id=1, replica_groups=mesh['groups'=2,'blk'=4,'draw'=2,'sub'=2] {'blk','sub'}, dimensions={0}, use_global_device_ids=true | all-gather | bytes 294912 | tf_op jit(solution)/shard_map/all_gather | solution.py:21
  32.8 0.6 gather_fusion.4
  33.4 1.2 %gather_fusion.3 = bf16[8,64,128]{2,1,0:T(8,128)(2,1)} fusion(bf16[16,64,128]{2,1,0:T(8,128)(2,1)S(1)} %all_gather.16, s32[1024]{0:T(1024)S(1)} %pad_clamp_fusion.6), kind=kCustom, calls=%fused_computation.1.clone | custom fusion | bytes 262176 | tf_op jit(solution)/shard_map/jit(_take)/gather | solution.py:11
  34.6 0.0 copy-done.5
  34.6 14.2 %all_gather.15 = bf16[16,64,128]{2,1,0:T(8,128)(2,1)S(1)} all-gather(bf16[2,64,128]{2,1,0:T(8,128)(2,1)S(1)} %copy-done.5), channel_id=1, replica_groups=mesh['groups'=2,'blk'=4,'draw'=2,'sub'=2] {'blk','sub'}, dimensions={0}, use_global_device_ids=true | all-gather | bytes 294912 | tf_op jit(solution)/shard_map/all_gather | solution.py:21
  48.8 0.0 copy-done.1
  48.8 0.2 slice_bitcast_fusion.3
  49.0 0.0 copy-start.2
  49.0 0.0 copy-start.3
  49.0 0.6 gather_fusion.2
  49.6 1.1 convolution_bitcast_fusion.7
  50.7 1.2 %convolution_convert_fusion.3 = bf16[2,64,128]{2,1,0:T(8,128)(2,1)S(1)} fusion(f32[2,64,128]{2,1,0:T(8,128)S(1)} %convolution_bitcast_fusion.7, bf16[2,6,128,128]{3,2,1,0:T(8,128)(2,1)S(1)} %get-tuple-element.11, bf16[2,2,64,128]{3,2,1,0:T(8,128)(2,1)S(1)} %bitcast.144, bf16[4,2,128,128]{3,2,1,0:T(8,128)(2,1)} %param.13, f32[4,2,64,128]{3,2,1,0:T(8,128)} %param.11, ...), kind=kOutput, calls=%fused_computation.34 | convolution fusion | flops 12681216 | bytes 426496 | tf_op jit(solution)/shard_map/bfp,bpq->bfq/dot_general | solution.py:45
  51.9 14.2 %all_gather.17 = bf16[16,64,128]{2,1,0:T(8,128)(2,1)S(1)} all-gather(bf16[2,64,128]{2,1,0:T(8,128)(2,1)S(1)} %convolution_convert_fusion.3), channel_id=1, replica_groups=mesh['groups'=2,'blk'=4,'draw'=2,'sub'=2] {'blk','sub'}, dimensions={0}, use_global_device_ids=true | all-gather | bytes 294912 | tf_op jit(solution)/shard_map/all_gather | solution.py:21
  66.2 0.6 gather_fusion.6
  66.7 0.6 gather_fusion.5
  67.3 0.2 convolution_bitcast_fusion.6
  67.5 0.0 copy-done.2
  67.6 0.3 convolution_convert_fusion.2
  67.9 14.2 %all_gather.18 = bf16[16,64,128]{2,1,0:T(8,128)(2,1)S(1)} all-gather(bf16[2,64,128]{2,1,0:T(8,128)(2,1)S(1)} %convolution_convert_fusion.2), channel_id=1, replica_groups=mesh['groups'=2,'blk'=4,'draw'=2,'sub'=2] {'blk','sub'}, dimensions={0}, use_global_device_ids=true | all-gather | bytes 294912 | tf_op jit(solution)/shard_map/all_gather | solution.py:21
  82.1 0.6 gather_fusion.8
  82.7 0.6 gather_fusion.7
  83.3 0.2 convolution_bitcast_fusion.5
  83.5 0.3 convolution_convert_fusion.1
  83.8 14.2 %all_gather.19 = bf16[16,64,128]{2,1,0:T(8,128)(2,1)S(1)} all-gather(bf16[2,64,128]{2,1,0:T(8,128)(2,1)S(1)} %convolution_convert_fusion.1), channel_id=1, replica_groups=mesh['groups'=2,'blk'=4,'draw'=2,'sub'=2] {'blk','sub'}, dimensions={0}, use_global_device_ids=true | all-gather | bytes 294912 | tf_op jit(solution)/shard_map/all_gather | solution.py:21
  98.1 0.6 gather_fusion.9
  98.6 0.2 convolution_bitcast_fusion.4
  98.9 0.3 fusion.12
  99.2 0.2 copy.30
  99.4 3.2 %gather_fusion.1 = bf16[1024,64]{1,0:T(8,128)(2,1)S(1)} fusion(bf16[64,1024]{0,1:T(8,128)(2,1)S(1)} %bitcast.136, s32[1024]{0:T(1024)S(1)} %fusion.80), kind=kCustom, calls=%fused_computation.9 | custom fusion | bytes 266240 | tf_op jit(solution)/shard_map/jit(_take)/gather | solution.py:56
  102.6 0.1 copy.18
  102.8 0.7 broadcast_select_fusion
  103.4 0.0 all-to-all-done
  103.4 4.6 %all-to-all-start.1 = ((bf16[64,8,128]{2,0,1:T(8,128)(2,1)}), bf16[64,8,128]{2,0,1:T(8,128)(2,1)S(1)}, u32[]{:S(2)}, u32[]{:S(2)}) async-start(bf16[64,8,128]{2,0,1:T(8,128)(2,1)} %broadcast_select_fusion), calls=%async_computation.1 | async-start | bytes 262144 | tf_op jit(solution)/shard_map/all_to_all | solution.py:57
  108.1 6.8 %all-to-all-done.1 = bf16[64,8,128]{2,0,1:T(8,128)(2,1)S(1)} async-done(((bf16[64,8,128]{2,0,1:T(8,128)(2,1)}), bf16[64,8,128]{2,0,1:T(8,128)(2,1)S(1)}, u32[]{:S(2)}, u32[]{:S(2)}) %all-to-all-start.1) | async-done | bytes 131104 | tf_op jit(solution)/shard_map/all_to_all | solution.py:57
  114.8 0.2 copy.20
  115.0 3.2 %scatter_custom_fusion = bf16[64,1024]{0,1:T(8,128)(2,1)S(1)} fusion(s32[1024]{0:T(1024)S(1)} %bitcast.150, bf16[1024,64]{1,0:T(8,128)(2,1)S(1)} %copy.20, bf16[]{:T(256)} %constant.52.clone.1), kind=kCustom, calls=%fused_computation.54 | custom fusion | bytes 131074 | tf_op jit(solution)/shard_map/scatter | solution.py:60
  118.2 0.8 copy.21
  (24 shorter events, 0.2 us)
Async XLA Ops:
  0.0 5.1 %copy-start = (s32[1024]{0:T(1024)S(1)}, s32[1024]{0:T(1024)}, u32[]{:S(2)}) copy-start(s32[1024]{0:T(1024)} %param.17) | copy-start | bytes 12292
  5.1 11.5 %copy-start.6 = (s32[4,2,6]{2,1,0:T(2,128)S(1)}, s32[4,2,6]{2,1,0:T(2,128)}, u32[]{:S(2)}) copy-start(s32[4,2,6]{2,1,0:T(2,128)} %param.16) | copy-start | bytes 580
  5.1 12.9 %copy-start.4 = (bf16[2,64,128]{2,1,0:T(8,128)(2,1)S(1)}, bf16[2,64,128]{2,1,0:T(8,128)(2,1)}, u32[]{:S(2)}) copy-start(bf16[2,64,128]{2,1,0:T(8,128)(2,1)} %param.15) | copy-start | bytes 98308
  5.2 29.4 %copy-start.5 = (bf16[2,64,128]{2,1,0:T(8,128)(2,1)S(1)}, bf16[2,64,128]{2,1,0:T(8,128)(2,1)}, u32[]{:S(2)}) copy-start(bf16[2,64,128]{2,1,0:T(8,128)(2,1)} %param.14) | copy-start | bytes 98308
  5.2 43.6 %copy-start.1 = (bf16[4,2,6,128,128]{4,3,2,1,0:T(8,128)(2,1)S(1)}, bf16[4,2,6,128,128]{4,3,2,1,0:T(8,128)(2,1)}, u32[]{:S(2)}) copy-start(bf16[4,2,6,128,128]{4,3,2,1,0:T(8,128)(2,1)} %param.12) | copy-start | bytes 4718596
  10.3 93.1 %all-to-all-start = ((s32[8,1,128]{2,1,0:T(1,128)}), s32[8,1,128]{2,1,0:T(1,128)S(1)}, u32[]{:S(2)}, u32[]{:S(2)}) async-start(s32[8,1,128]{2,1,0:T(1,128)} %bitcast), calls=%async_computation | async-start | bytes 8192 | tf_op jit(solution)/shard_map/all_to_all | solution.py:53
  49.0 18.5 %copy-start.2 = (bf16[4,2,128,128]{3,2,1,0:T(8,128)(2,1)S(1)}, bf16[4,2,128,128]{3,2,1,0:T(8,128)(2,1)}, u32[]{:S(2)}) copy-start(bf16[4,2,128,128]{3,2,1,0:T(8,128)(2,1)} %param.13) | copy-start | bytes 786436
  49.0 18.5 %copy-start.3 = (f32[4,2,64,128]{3,2,1,0:T(8,128)S(1)}, f32[4,2,64,128]{3,2,1,0:T(8,128)}, u32[]{:S(2)}) copy-start(f32[4,2,64,128]{3,2,1,0:T(8,128)} %param.11) | copy-start | bytes 786436
  103.4 11.4 %all-to-all-start.1 = ((bf16[64,8,128]{2,0,1:T(8,128)(2,1)}), bf16[64,8,128]{2,0,1:T(8,128)(2,1)S(1)}, u32[]{:S(2)}, u32[]{:S(2)}) async-start(bf16[64,8,128]{2,0,1:T(8,128)(2,1)} %broadcast_select_fusion), calls=%async_computation.1 | async-start | bytes 262144 | tf_op jit(solution)/shard_map/all_to_all | solution.py:57
where the time goes:
time: 119 us
  blocking collectives  71.6 us (60%)
  local copies, waits for them, and re-layouts  18.3 us (15%)
  starting transfers between devices  10.9 us (9%)
  other arithmetic  7.13 us (6%)
  waiting for transfers between devices  6.76 us (6%)
  matrix products  4.01 us (3%)
    all_gather x5, blocking collectives, share_section(): gathered = lax.all_gather(solved, ('blk', 'sub'), axis=0, tiled=True)  71.6 us
    all_to_all x1, waiting for transfers between devices, shards(): lax.all_to_all(moving, ('blk', 'sub'), split_axis=1, concat_axis=1, tiled...  6.76 us
    all_to_all x1, starting transfers between devices, shards(): lax.all_to_all(sorted_spots, ('blk', 'sub'), split_axis=0, concat_axis=0,...  6.33 us
    gather x8, local copies, waits for them, and re-layouts, lookup(): return jnp.take(gathered, neighbour_ids, axis=0)  5.18 us
    sort x1, other arithmetic, shards(): ordering = jnp.argsort(spot_map)  5.12 us
    all_to_all x1, starting transfers between devices, shards(): lax.all_to_all(moving, ('blk', 'sub'), split_axis=1, concat_axis=1, tiled...  4.58 us
    gather x1, local copies, waits for them, and re-layouts, shards(): sorted_spots = jnp.take(spot_map, ordering).reshape(owners, per_pair)  4.53 us
    scatter x2, local copies, waits for them, and re-layouts, shards(): result.at[:, spot_local].set(arrived.reshape(draw_count, point_count))  4.01 us
  transfers between devices with their start and end apart: 2, of which 1 were waited for; matrix products, arithmetic and copies ran while one was open for 13% of the time, Pallas kernels for 0%

commit v1 on v0

v1 whole, which is shorter than its diff:
```python
import functools

import jax
import jax.numpy as jnp
from jax import lax
from jax.experimental import pallas as pl
from jax.experimental.pallas import tpu as pltpu
from jax.sharding import PartitionSpec as P

K1 = 4
HALVES = 2
LANES = 128
OWN = ("blk", "sub")
MESH = pl.DeviceIdType.MESH
F32 = jnp.float32
BF16 = jnp.bfloat16


def repeat(count, body):
    if count <= 8:
        for at in range(count):
            body(at)
    else:
        pl.loop(0, count)(body)


def sweep(
    dims, regroup, neigh, spots, white_hbm, coup_hbm, diag_hbm, far, near, out,
    white, coup, diag, pool, flat, place, unplace, moved, landed, pos_out, pos_in, total,
    load_sem, own_sem, send_sem, hop_sem, recv_sem, pos_send, pos_recv, move_send, move_recv,
):
    blks, subs, levels, lb, draws, neighs = dims
    owners = blks * subs
    z, c = lax.axis_index("blk"), lax.axis_index("sub")
    me = z * subs + c
    half = draws // HALVES

    def device(owner):
        return {"blk": owner // subs, "sub": lax.rem(owner, subs)}

    def peer(step):
        return lax.rem(me + step, owners)

    def ahead(step):
        return lax.rem(z + step, blks)

    mates = subs - 1

    loads = [
        pltpu.make_async_copy(src, dst, load_sem.at[i])
        for i, (src, dst) in enumerate(((coup_hbm, coup), (white_hbm, white), (diag_hbm, diag)))
    ]
    for load in loads:
        load.start()

    def mine(sec, h):
        return pool[sec][h].at[pl.ds(me * lb, lb)]

    def section_of(sec, h):
        if sec < 2:
            ref = (far, near)[sec]
            return ref.at[:, pl.ds(h * half, half), :]
        return mine(sec, h)

    def own_copy(sec, h):
        return pltpu.make_async_copy(section_of(sec, h), mine(sec, h), own_sem.at[sec, h])

    def along(sec, h, step):
        return pltpu.make_async_remote_copy(
            section_of(sec, h), mine(sec, h), send_sem.at[sec, h, step], recv_sem.at[sec, h, me],
            device_id={"blk": ahead(step), "sub": c}, device_id_type=MESH)

    def across(sec, h):
        return pltpu.make_async_remote_copy(
            section_of(sec, h), mine(sec, h), send_sem.at[sec, h, 0], recv_sem.at[sec, h, me],
            device_id={"sub": mates - c}, device_id_type=MESH)

    def relay(sec, h, step):
        owner = lax.rem(z + blks - step, blks) * subs + c
        slot = pool[sec][h].at[pl.ds(owner * lb, lb)]
        return pltpu.make_async_remote_copy(
            slot, slot, hop_sem.at[sec, h, step], recv_sem.at[sec, h, owner],
            device_id={"sub": mates - c}, device_id_type=MESH)

    def arrival(sec, h, owner):
        slot = pool[sec][h].at[pl.ds(owner * lb, lb)]
        return pltpu.make_async_remote_copy(
            slot, slot, hop_sem.at[sec, h, 0], recv_sem.at[sec, h, owner],
            device_id={"sub": mates - c}, device_id_type=MESH)

    def share(sec, h):
        repeat(blks - 1, lambda i: along(sec, h, i + 1).start())
        across(sec, h).start()

    def collect(secs, h):
        for sec in secs:
            def pass_on(i, sec=sec):
                owner = lax.rem(z + blks - (i + 1), blks) * subs + c
                arrival(sec, h, owner).wait_recv()
                relay(sec, h, i + 1).start()
            repeat(blks - 1, pass_on)
        for sec in secs:
            def take(i, sec=sec):
                owner = lax.rem(z + blks - i, blks) * subs + mates - c
                arrival(sec, h, owner).wait_recv()
            repeat(blks, take)

    barrier = pltpu.get_barrier_semaphore()
    repeat(owners - 1, lambda i: pl.semaphore_signal(
        barrier, inc=1, device_id=device(peer(i + 1)), device_id_type=MESH))
    for h in range(HALVES):
        for sec in (1, 0):
            own_copy(sec, h).start()
    pl.semaphore_wait(barrier, owners - 1)
    for h in range(HALVES):
        for sec in (1, 0):
            share(sec, h)

    chunks = levels * lb
    points = chunks * LANES
    place_of = lambda: lax.broadcasted_iota(jnp.int32, (LANES, points), 1).astype(F32)

    def pos_copy(step):
        to = peer(step)
        return pltpu.make_async_remote_copy(
            pos_out.at[to], pos_in.at[me], pos_send.at[step], pos_recv.at[me],
            device_id=device(to), device_id_type=MESH)

    def pos_arrival(owner):
        return pltpu.make_async_remote_copy(
            pos_out.at[owner], pos_in.at[owner], pos_send.at[0], pos_recv.at[owner],
            device_id=device(peer(1)), device_id_type=MESH)

    def move_copy(step):
        to = peer(step)
        return pltpu.make_async_remote_copy(
            moved.at[to], landed.at[me], move_send.at[step], move_recv.at[me],
            device_id=device(to), device_id_type=MESH)

    def move_arrival(owner):
        return pltpu.make_async_remote_copy(
            moved.at[owner], landed.at[owner], move_send.at[0], move_recv.at[owner],
            device_id=device(peer(1)), device_id_type=MESH)

    def rank_points():
        spot = spots[...]
        rows = spot.astype(F32)
        cols = rows.T
        local = lax.rem(spot, points).astype(F32).T
        lane = place_of()
        ordered = jnp.zeros((1, points), F32)
        for k in range(chunks):
            col = cols[:, k:k + 1]
            below = jnp.zeros((LANES, LANES), F32)
            for j in range(chunks):
                below += jnp.where(rows[j:j + 1, :] < col, 1.0, 0.0)
            rank = jnp.sum(below, axis=1, keepdims=True)
            hit = lane == rank
            place[k * LANES:(k + 1) * LANES, :] = jnp.where(hit, 1.0, 0.0).astype(BF16)
            ordered += jnp.sum(jnp.where(hit, local[:, k:k + 1], 0.0), axis=0, keepdims=True)
        for s in range(owners):
            pos_out[s] = jnp.broadcast_to(ordered[:, s * LANES:(s + 1) * LANES], (8, LANES))
        for i in range(1, owners):
            pos_copy(i).start()
        pos_in[me] = pos_out[me]

    def place_arrivals():
        lane = place_of()
        for i in range(1, owners):
            pos_arrival(peer(i)).wait_recv()
        for o in range(owners):
            col = pos_in[o].T[:, 0:1]
            unplace[o * LANES:(o + 1) * LANES, :] = jnp.where(lane == col, 1.0, 0.0).astype(BF16)

    if regroup:
        rank_points()

    for h in range(HALVES):
        for sec in (1, 0):
            own_copy(sec, h).wait()
    for load in loads:
        load.wait()

    def tiles(level, b, h, sec, first, last):
        rows = jnp.concatenate([pool[sec][h][neigh[level, b, k]] for k in range(first, last)], axis=1)
        factor = coup[level, b, first:last].reshape((last - first) * LANES, LANES)
        return jnp.dot(rows, factor, preferred_element_type=F32)

    for level in range(levels):
        for h in range(HALVES):
            if level == 0:
                collect((1, 0), h)
            rest = [
                white[level, b, h * half:(h + 1) * half, :] - tiles(level, b, h, level, K1, neighs)
                for b in range(lb)
            ]
            if level > 0:
                collect((level + 1,), h)
            for b in range(lb):
                remain = (rest[b] - tiles(level, b, h, level + 1, 0, K1)).astype(BF16)
                solved = jnp.dot(remain, diag[level, b], preferred_element_type=F32).astype(BF16)
                flat[level * lb + b, h * half:(h + 1) * half, :] = solved
                if level + 1 < levels:
                    pool[level + 2][h][me * lb + b] = solved
            if level + 1 < levels:
                share(level + 2, h)
        if regroup:
            part = sum(
                jnp.dot(flat[k], place[k * LANES:(k + 1) * LANES, :], preferred_element_type=F32)
                for k in range(level * lb, (level + 1) * lb)
            )
            if level == 0:
                total[...] = part
                place_arrivals()
            elif level + 1 < levels:
                total[...] += part
            else:
                final = (total[...] + part).astype(BF16)
                for s in range(owners):
                    moved[s] = final[:, s * LANES:(s + 1) * LANES]
                for i in range(1, owners):
                    move_copy(i).start()

    if regroup:
        def laid(ref, o):
            return jnp.dot(ref[o], unplace[pl.ds(pl.multiple_of(o * LANES, LANES), LANES), :],
                           preferred_element_type=F32)

        total[...] = laid(moved, me)
        for i in range(1, owners):
            owner = peer(i)
            move_arrival(owner).wait_recv()
            total[...] += laid(landed, owner)
        out[...] = total[...].astype(BF16)
        for i in range(1, owners):
            pos_copy(i).wait_send()
            move_copy(i).wait_send()
    else:
        out[...] = flat[...]
    for sec in range(levels + 1):
        for h in range(HALVES):
            def sent(i, sec=sec, h=h):
                along(sec, h, i + 1).wait_send()
                relay(sec, h, i + 1).wait_send()
            repeat(blks - 1, sent)
            across(sec, h).wait_send()


def shards(white_noise, coupling, diag_inv, prior_far, prior_near, neighbours, spot_map):
    blks, subs = lax.axis_size("blk"), lax.axis_size("sub")
    owners = blks * subs
    levels, lb, draws, size = white_noise.shape
    points = spot_map.shape[0]
    per_pair = points // owners
    regroup = per_pair == LANES
    chunks = levels * lb
    secs = levels + 1
    dims = (blks, subs, levels, lb, draws, neighbours.shape[2])
    out_shape = (draws, points) if regroup else (chunks, draws, size)
    dma = pltpu.SemaphoreType.DMA
    vmem, smem = pl.BlockSpec(memory_space=pltpu.VMEM), pl.BlockSpec(memory_space=pltpu.SMEM)
    anywhere = pl.BlockSpec(memory_space=pl.ANY)
    pairs = owners if regroup else 1
    flops = 2 * draws * size * size * chunks * 7 + 4 * draws * points * points
    result = pl.pallas_call(
        functools.partial(sweep, dims, regroup),
        out_shape=jax.ShapeDtypeStruct(out_shape, BF16),
        in_specs=[smem, vmem] + [anywhere] * 5,
        out_specs=vmem,
        scratch_shapes=[
            pltpu.VMEM(white_noise.shape, F32),
            pltpu.VMEM(coupling.shape, BF16),
            pltpu.VMEM(diag_inv.shape, BF16),
            [[pltpu.VMEM((owners * lb, draws // HALVES, size), BF16)] * HALVES] * secs,
            pltpu.VMEM((chunks, draws, size), BF16),
            pltpu.VMEM((points, points), BF16),
            pltpu.VMEM((points, points), BF16),
            pltpu.VMEM((pairs, draws, LANES), BF16),
            pltpu.VMEM((pairs, draws, LANES), BF16),
            pltpu.VMEM((pairs, 8, LANES), F32),
            pltpu.VMEM((pairs, 8, LANES), F32),
            pltpu.VMEM((draws, points), F32),
            dma((3,)),
            dma((2, HALVES)),
            dma((secs, HALVES, blks)),
            dma((secs, HALVES, blks)),
            dma((secs, HALVES, owners)),
            dma((owners,)),
            dma((owners,)),
            dma((owners,)),
            dma((owners,)),
        ],
        compiler_params=pltpu.CompilerParams(
            collective_id=0, has_side_effects=True, vmem_limit_bytes=48 * 1024 * 1024),
        cost_estimate=pl.CostEstimate(flops=flops, bytes_accessed=3 * 2**20, transcendentals=0),
    )(neighbours, spot_map.reshape(points // LANES, LANES), white_noise, coupling, diag_inv,
      prior_far, prior_near)
    if regroup:
        return result
    ordering = jnp.argsort(spot_map)
    sorted_spots = jnp.take(spot_map, ordering).reshape(owners, per_pair)
    placings = lax.all_to_all(sorted_spots, OWN, split_axis=0, concat_axis=0, tiled=True)
    local = result.transpose(1, 0, 2).reshape(draws, points)
    moving = jnp.take(local, ordering, axis=1).reshape(draws, owners, per_pair)
    arrived = lax.all_to_all(moving, OWN, split_axis=1, concat_axis=1, tiled=True)
    spot_local = placings.reshape(-1) % points
    return jnp.zeros((draws, points), BF16).at[:, spot_local].set(arrived.reshape(draws, points))


def solution(mesh):
    return jax.shard_map(
        shards,
        mesh=mesh,
        in_specs=(
            P(None, ("groups", "blk", "sub"), "draw", None),
            P(None, ("groups", "blk", "sub"), None, None, None),
            P(None, ("groups", "blk", "sub"), None, None),
            P(("groups", "blk", "sub"), "draw", None),
            P(("groups", "blk", "sub"), "draw", None),
            P(None, ("groups", "blk", "sub"), None),
            P(("groups", "blk", "sub")),
        ),
        out_specs=P("draw", ("groups", "blk", "sub")),
        check_vma=False,
    )
```

time: 119 us -> 42.9 us (0.36)
  blocking collectives: 71.6 us -> 0 us
  Pallas kernels: 0 us -> 35.4 us
  local copies, waits for them, and re-layouts: 18.3 us -> 6.85 us
  starting transfers between devices: 10.9 us -> 0 us
  other arithmetic: 7.13 us -> 0 us
  waiting for transfers between devices: 6.76 us -> 0 us
  matrix products: 4.01 us -> 0 us
    all_gather x5 -> x0, blocking collectives: 71.6 us -> none  [share_section(): gathered = lax.all_gather(solved, ('blk', 'sub'), axis=0, tiled=True)]
    pallas_call x0 -> x1, Pallas kernels: none -> 35.4 us  [shards(): pl.pallas_call(functools.partial(sweep, dims, regroup), out_shape=jax.Sha...]
    gather x11 -> x0, local copies, waits for them, and re-layouts: 13.1 us -> none  [the longest x8 5.18 us: lookup(): return jnp.take(gathered, neighbour_ids, axis=0)]
    all_to_all x2 -> x0, starting transfers between devices: 10.9 us -> none  [the longest x1 6.33 us: shards(): lax.all_to_all(sorted_spots, ('blk', 'sub'), split_axis=0, concat_axis=0,...]
    unnamed x14 -> x15, local copies, waits for them, and re-layouts: 0.04 us -> 6.85 us
    all_to_all x2 -> x0, waiting for transfers between devices: 6.76 us -> none  [the longest x1 6.76 us: shards(): lax.all_to_all(moving, ('blk', 'sub'), split_axis=1, concat_axis=1, tiled...]
    sort x1 -> x0, other arithmetic: 5.12 us -> none  [shards(): ordering = jnp.argsort(spot_map)]
    scatter x2 -> x0, local copies, waits for them, and re-layouts: 4.01 us -> none  [shards(): result.at[:, spot_local].set(arrived.reshape(draw_count, point_count))]
  transfers between devices with their start and end apart: 2 -> 0, of which waited for: 1 -> 0; matrix products, arithmetic and copies ran while one was open for 13% -> 0% of each run, Pallas kernels for 0% -> 0%
where the time goes in v1:
time: 42.9 us; the launch traced here: 42.2 us
  Pallas kernels  35.4 us (83%)
  local copies, waits for them, and re-layouts  6.85 us (16%)
    pallas_call x1, Pallas kernels, shards(): pl.pallas_call(functools.partial(sweep, dims, regroup), out_shape=jax.Sha...  35.4 us
    unnamed x15, local copies, waits for them, and re-layouts  6.85 us

profile of v1, /device:TPU:0, one launch (start us, length us, event | category | flops | bytes accessed | tf_op | source)
XLA Modules:
  0.0 42.2 jit_solution(11131864599791088138)
XLA Ops:
  0.0 0.0 copy-start
  0.0 1.4 %copy-done = bf16[4,2,6,128,128]{4,3,2,1,0:T(8,128)(2,1)S(1)} copy-done((bf16[4,2,6,128,128]{4,3,2,1,0:T(8,128)(2,1)S(1)}, bf16[4,2,6,128,128]{4,3,2,1,0:T(8,128)(2,1)}, u32[]{:S(2)}) %copy-start) | copy-done | bytes 1572888
  1.4 0.0 copy-start.1
  1.4 0.9 %copy-done.1 = f32[4,2,64,128]{3,2,1,0:T(8,128)S(1)} copy-done((f32[4,2,64,128]{3,2,1,0:T(8,128)S(1)}, f32[4,2,64,128]{3,2,1,0:T(8,128)}, u32[]{:S(2)}) %copy-start.1) | copy-done | bytes 262168
  2.4 0.0 copy-start.2
  2.4 0.9 %copy-done.2 = bf16[4,2,128,128]{3,2,1,0:T(8,128)(2,1)S(1)} copy-done((bf16[4,2,128,128]{3,2,1,0:T(8,128)(2,1)S(1)}, bf16[4,2,128,128]{3,2,1,0:T(8,128)(2,1)}, u32[]{:S(2)}) %copy-start.2) | copy-done | bytes 262168
  3.3 0.0 copy-start.3
  3.3 0.8 %copy-done.3 = bf16[2,64,128]{2,1,0:T(8,128)(2,1)S(1)} copy-done((bf16[2,64,128]{2,1,0:T(8,128)(2,1)S(1)}, bf16[2,64,128]{2,1,0:T(8,128)(2,1)}, u32[]{:S(2)}) %copy-start.3) | copy-done | bytes 32792
  4.1 0.0 copy-start.4
  4.1 0.8 %copy-done.4 = bf16[2,64,128]{2,1,0:T(8,128)(2,1)S(1)} copy-done((bf16[2,64,128]{2,1,0:T(8,128)(2,1)S(1)}, bf16[2,64,128]{2,1,0:T(8,128)(2,1)}, u32[]{:S(2)}) %copy-start.4) | copy-done | bytes 32792
  4.8 0.0 copy-start.5
  4.8 0.7 %copy-done.5 = s32[4,2,6]{2,1,0:T(2,128)S(1)} copy-done((s32[4,2,6]{2,1,0:T(2,128)S(1)}, s32[4,2,6]{2,1,0:T(2,128)}, u32[]{:S(2)}) %copy-start.5) | copy-done | bytes 216
  5.5 0.0 copy-start.6
  5.5 0.7 %copy-done.6 = s32[1024]{0:T(1024)S(1)} copy-done((s32[1024]{0:T(1024)S(1)}, s32[1024]{0:T(1024)}, u32[]{:S(2)}) %copy-start.6) | copy-done | bytes 4120
  6.2 35.4 %shard_map.73 = bf16[64,1024]{1,0:T(8,128)(2,1)S(1)} custom-call(s32[4,2,6]{2,1,0:T(2,128)S(1)} %copy-done.5, s32[8,128]{1,0:T(8,128)S(1)} %bitcast.1, f32[4,2,64,128]{3,2,1,0:T(8,128)S(1)} %copy-done.1, bf16[4,2,6,128,128]{4,3,2,1,0:T(8,128)(2,1)S(1)} %copy-done, bf16[4,2,128,128]{3,2,1,0:T(8,128)(2,1)S(1)} %copy-done.2, bf16[2,64,128]{2,1,0:T(8,128)(2,1)S(1)} %copy-done.3, ...), custom_call_target="tpu_custom_call" | custom-call | flops 385875968 | bytes 3145728 | tf_op jit(solution)/shard_map/pallas_call | solution.py:265
  41.6 0.7 %copy.9 = bf16[64,1024]{1,0:T(8,128)(2,1)} copy(bf16[64,1024]{1,0:T(8,128)(2,1)S(1)} %shard_map.73) | data formatting | bytes 262144
Async XLA Ops:
  0.0 1.4 %copy-start = (bf16[4,2,6,128,128]{4,3,2,1,0:T(8,128)(2,1)S(1)}, bf16[4,2,6,128,128]{4,3,2,1,0:T(8,128)(2,1)}, u32[]{:S(2)}) copy-start(bf16[4,2,6,128,128]{4,3,2,1,0:T(8,128)(2,1)} %coup_hbm.1) | copy-start | bytes 4718596
  1.4 0.9 %copy-start.1 = (f32[4,2,64,128]{3,2,1,0:T(8,128)S(1)}, f32[4,2,64,128]{3,2,1,0:T(8,128)}, u32[]{:S(2)}) copy-start(f32[4,2,64,128]{3,2,1,0:T(8,128)} %white_hbm.1) | copy-start | bytes 786436
  2.4 0.9 %copy-start.2 = (bf16[4,2,128,128]{3,2,1,0:T(8,128)(2,1)S(1)}, bf16[4,2,128,128]{3,2,1,0:T(8,128)(2,1)}, u32[]{:S(2)}) copy-start(bf16[4,2,128,128]{3,2,1,0:T(8,128)(2,1)} %diag_hbm.1) | copy-start | bytes 786436
  3.3 0.8 %copy-start.3 = (bf16[2,64,128]{2,1,0:T(8,128)(2,1)S(1)}, bf16[2,64,128]{2,1,0:T(8,128)(2,1)}, u32[]{:S(2)}) copy-start(bf16[2,64,128]{2,1,0:T(8,128)(2,1)} %far.1) | copy-start | bytes 98308
  4.1 0.8 %copy-start.4 = (bf16[2,64,128]{2,1,0:T(8,128)(2,1)S(1)}, bf16[2,64,128]{2,1,0:T(8,128)(2,1)}, u32[]{:S(2)}) copy-start(bf16[2,64,128]{2,1,0:T(8,128)(2,1)} %near.1) | copy-start | bytes 98308
  4.8 0.7 %copy-start.5 = (s32[4,2,6]{2,1,0:T(2,128)S(1)}, s32[4,2,6]{2,1,0:T(2,128)}, u32[]{:S(2)}) copy-start(s32[4,2,6]{2,1,0:T(2,128)} %neigh.1) | copy-start | bytes 580
  5.5 0.7 %copy-start.6 = (s32[1024]{0:T(1024)S(1)}, s32[1024]{0:T(1024)}, u32[]{:S(2)}) copy-start(s32[1024]{0:T(1024)} %param.13) | copy-start | bytes 12292

commit v2 on v0

v2 whole, which is shorter than its diff:
```python
import functools

import jax
import jax.numpy as jnp
from jax import lax
from jax.experimental import pallas as pl
from jax.experimental.pallas import tpu as pltpu
from jax.sharding import PartitionSpec as P

K1 = 4
HALVES = 2
LANES = 128
OWN = ("blk", "sub")
MESH = pl.DeviceIdType.MESH
F32 = jnp.float32
BF16 = jnp.bfloat16


def repeat(count, body):
    if count <= 8:
        for at in range(count):
            body(at)
    else:
        pl.loop(0, count)(body)


def sweep(
    dims, regroup, neigh_hbm, spots_hbm, white_hbm, coup_hbm, diag_hbm, far, near, out,
    neigh, neigh_vm, spots, white, coup, diag, pool, flat, place, unplace, moved, landed,
    pos_out, pos_in, total, load_sem, push_send, push_recv, smem_sem, own_sem, prior_send,
    prior_recv, level_send, level_recv, pos_send, pos_recv, move_send, move_recv, stay_sem,
):
    blks, subs, levels, lb, draws, neighs = dims
    owners = blks * subs
    z, c = lax.axis_index("blk"), lax.axis_index("sub")
    me = z * subs + c
    mate = subs - 1 - c
    share_of = draws // subs
    half = share_of // HALVES
    chunks = levels * lb
    points = spots.shape[1] * LANES

    def device(owner):
        return {"blk": owner // subs, "sub": lax.rem(owner, subs)}

    def peer(step):
        return lax.rem(me + step, owners)

    def chip(step):
        return lax.rem(z + step, blks)

    def rows_of(core):
        return pl.ds(pl.multiple_of(core * share_of, share_of), share_of)

    wares = [(spots_hbm, spots.at[c]), (neigh_hbm, neigh_vm.at[c])]
    wares += [(coup_hbm.at[0], coup.at[c, 0]), (diag_hbm, diag.at[c])]
    wares += [(coup_hbm.at[i], coup.at[c, i]) for i in range(1, levels)]
    noise_at = len(wares)

    def load(i):
        src, dst = wares[i]
        return pltpu.make_async_copy(src, dst, load_sem.at[i])

    def push(i):
        src, dst = wares[i]
        return pltpu.make_async_remote_copy(
            src, dst, push_send.at[i], push_recv.at[i], device_id={"sub": mate}, device_id_type=MESH)

    def load_noise():
        return pltpu.make_async_copy(
            white_hbm.at[:, :, rows_of(c), :], white.at[c], load_sem.at[noise_at])

    def push_noise():
        return pltpu.make_async_remote_copy(
            white_hbm.at[:, :, rows_of(mate), :], white.at[c], push_send.at[noise_at],
            push_recv.at[noise_at], device_id={"sub": mate}, device_id_type=MESH)

    def ready(i):
        load(i).wait()
        push(i).wait_recv()

    priors = (far, near)

    def prior_rows(sec, h, core):
        return priors[sec].at[:, pl.ds(pl.multiple_of(core * share_of + h * half, half), half), :]

    def prior_slot(sec, h, owner):
        return pool[sec][h].at[pl.ds(owner * lb, lb)]

    def prior_stay(sec, h):
        return pltpu.make_async_copy(prior_rows(sec, h, c), prior_slot(sec, h, me), own_sem.at[sec, h])

    def prior_copy(sec, h, step, core):
        return pltpu.make_async_remote_copy(
            prior_rows(sec, h, core), prior_slot(sec, h, me), prior_send.at[sec, h, step, core],
            prior_recv.at[sec, h, me], device_id={"blk": chip(step), "sub": core}, device_id_type=MESH)

    def prior_across(sec, h):
        return pltpu.make_async_remote_copy(
            prior_rows(sec, h, mate), prior_slot(sec, h, me), prior_send.at[sec, h, 0, 0],
            prior_recv.at[sec, h, me], device_id={"sub": mate}, device_id_type=MESH)

    def prior_arrival(sec, h, owner):
        slot = prior_slot(sec, h, owner)
        return pltpu.make_async_remote_copy(
            slot, slot, prior_send.at[sec, h, 0, 0], prior_recv.at[sec, h, owner],
            device_id={"sub": mate}, device_id_type=MESH)

    def share_prior(sec, h):
        for core in range(subs):
            repeat(blks - 1, lambda i, core=core: prior_copy(sec, h, i + 1, core).start())
        prior_across(sec, h).start()

    def level_slot(sec, h, at):
        return pool[sec][h].at[pl.ds(at * (subs * lb), subs * lb)]

    def level_copy(sec, h, step):
        return pltpu.make_async_remote_copy(
            level_slot(sec, h, z), level_slot(sec, h, z), level_send.at[sec - 2, h, step],
            level_recv.at[sec - 2, h, z], device_id={"blk": chip(step), "sub": c}, device_id_type=MESH)

    def level_arrival(sec, h, at):
        return pltpu.make_async_remote_copy(
            level_slot(sec, h, at), level_slot(sec, h, at), level_send.at[sec - 2, h, 0],
            level_recv.at[sec - 2, h, at], device_id={"blk": chip(1), "sub": c}, device_id_type=MESH)

    def collect(sec, h):
        if sec < 2:
            prior_stay(sec, h).wait()
            repeat(owners - 1, lambda i: prior_arrival(sec, h, peer(i + 1)).wait_recv())
        else:
            repeat(blks - 1, lambda i: level_arrival(sec, h, chip(i + 1)).wait_recv())

    def pos_copy(step):
        to = peer(step)
        return pltpu.make_async_remote_copy(
            pos_out.at[to], pos_in.at[me], pos_send.at[step], pos_recv.at[me],
            device_id=device(to), device_id_type=MESH)

    def pos_arrival(owner):
        return pltpu.make_async_remote_copy(
            pos_out.at[owner], pos_in.at[owner], pos_send.at[0], pos_recv.at[owner],
            device_id=device(peer(1)), device_id_type=MESH)

    def landing(at, core):
        return landed.at[pl.ds(at * subs, subs), rows_of(core), :]

    def move_copy(step):
        to = peer(step)
        return pltpu.make_async_remote_copy(
            moved.at[to], landing(z, c), move_send.at[step], move_recv.at[me],
            device_id=device(to), device_id_type=MESH)

    def move_stay():
        return pltpu.make_async_copy(moved.at[me], landing(z, c), stay_sem.at[0])

    def move_arrival(at, core):
        owner = at * subs + core
        return pltpu.make_async_remote_copy(
            moved.at[owner], landing(at, core), move_send.at[0], move_recv.at[owner],
            device_id=device(peer(1)), device_id_type=MESH)

    def lane():
        return lax.broadcasted_iota(jnp.int32, (LANES, points), 1).astype(F32)

    def rank_points(owner, own):
        spot = spots[owner]
        rows = spot.astype(F32)
        cols = rows.T
        local = lax.rem(spot, points).astype(F32).T
        ordered = jnp.zeros((1, points), F32)
        for k in range(chunks):
            col = cols[:, k:k + 1]
            below = jnp.zeros((LANES, LANES), F32)
            for j in range(chunks):
                below += jnp.where(rows[j:j + 1, :] < col, 1.0, 0.0)
            rank = jnp.sum(below, axis=1, keepdims=True)
            hit = lane() == rank
            place[owner, k * LANES:(k + 1) * LANES, :] = jnp.where(hit, 1.0, 0.0).astype(BF16)
            if own:
                ordered += jnp.sum(jnp.where(hit, local[:, k:k + 1], 0.0), axis=0, keepdims=True)
        if own:
            for s in range(owners):
                pos_out[s] = jnp.broadcast_to(ordered[:, s * LANES:(s + 1) * LANES], (8, LANES))
            pos_in[me] = pos_out[me]

    def place_arrivals():
        for i in range(1, owners):
            pos_arrival(peer(i)).wait_recv()
        for o in range(owners):
            col = pos_in[o].T[:, 0:1]
            unplace[o * LANES:(o + 1) * LANES, :] = jnp.where(lane() == col, 1.0, 0.0).astype(BF16)

    barrier = pltpu.get_barrier_semaphore()
    repeat(owners - 1, lambda i: pl.semaphore_signal(
        barrier, inc=1, device_id=device(peer(i + 1)), device_id_type=MESH))
    for i in range(2):
        load(i).start()
    for h in range(HALVES):
        for sec in (1, 0):
            prior_stay(sec, h).start()
    for i in range(2, noise_at):
        load(i).start()
    load_noise().start()
    load(0).wait()
    if regroup:
        rank_points(c, True)
    pl.semaphore_wait(barrier, owners - 1)
    for sec in (1, 0):
        share_prior(sec, 0)
    for i in range(4):
        push(i).start()
    push_noise().start()
    for h in range(1, HALVES):
        for sec in (1, 0):
            share_prior(sec, h)
    for i in range(4, noise_at):
        push(i).start()
    if regroup:
        for i in range(1, owners):
            pos_copy(i).start()
    push(0).wait_recv()
    if regroup:
        rank_points(mate, False)
    ready(1)
    to_smem = pltpu.make_async_copy(neigh_vm, neigh, smem_sem.at[0])
    to_smem.start()
    to_smem.wait()
    load_noise().wait()
    push_noise().wait_recv()
    for i in (2, 3):
        ready(i)

    def tiles(level, o, b, h, sec, first, last):
        rows = jnp.concatenate([pool[sec][h][neigh[o, level, b, k]] for k in range(first, last)], axis=1)
        factor = coup[o, level, b, first:last].reshape((last - first) * LANES, LANES)
        return jnp.dot(rows, factor, preferred_element_type=F32)

    blocks = [(o, b) for o in range(subs) for b in range(lb)]
    for level in range(levels):
        if level > 0:
            ready(level + 3)
        for h in range(HALVES):
            span = slice(h * half, (h + 1) * half)
            if level == 0:
                collect(0, h)
            rest = [
                white[o, level, b, span, :] - tiles(level, o, b, h, level, K1, neighs)
                for o, b in blocks
            ]
            collect(level + 1, h)
            remain = [
                (r - tiles(level, o, b, h, level + 1, 0, K1)).astype(BF16)
                for r, (o, b) in zip(rest, blocks)
            ]
            for r, (o, b) in zip(remain, blocks):
                solved = jnp.dot(r, diag[o, level, b], preferred_element_type=F32).astype(BF16)
                flat[o, level * lb + b, span, :] = solved
                if level + 1 < levels:
                    pool[level + 2][h][z * (subs * lb) + o * lb + b] = solved
            if level + 1 < levels:
                repeat(blks - 1, lambda i: level_copy(level + 2, h, i + 1).start())
        if regroup:
            for o in range(subs):
                part = sum(
                    jnp.dot(flat[o, k], place[o, k * LANES:(k + 1) * LANES, :], preferred_element_type=F32)
                    for k in range(level * lb, (level + 1) * lb)
                )
                if level == 0:
                    total[o] = part
                elif level + 1 < levels:
                    total[o] += part
                else:
                    final = (total[o] + part).astype(BF16)
                    for s in range(owners):
                        moved[s, o] = final[:, s * LANES:(s + 1) * LANES]
            if level == 0:
                place_arrivals()

    if regroup:
        for i in range(1, owners):
            move_copy(i).start()
        move_stay().start()

        def laid(at):
            rows = jnp.concatenate([landed[at * subs + o] for o in range(subs)], axis=1)
            width = subs * LANES
            return jnp.dot(rows, unplace[pl.ds(pl.multiple_of(at * width, width), width), :],
                           preferred_element_type=F32)

        move_stay().wait()
        move_arrival(z, mate).wait_recv()
        whole = laid(z)
        for i in range(1, blks):
            for core in range(subs):
                move_arrival(chip(i), core).wait_recv()
            whole += laid(chip(i))
        out[...] = whole.astype(BF16)
        for i in range(1, owners):
            pos_copy(i).wait_send()
            move_copy(i).wait_send()
    else:
        out[...] = flat[...]
    for h in range(HALVES):
        for sec in range(2):
            for core in range(subs):
                repeat(blks - 1, lambda i: prior_copy(sec, h, i + 1, core).wait_send())
            prior_across(sec, h).wait_send()
        for sec in range(2, levels + 1):
            repeat(blks - 1, lambda i: level_copy(sec, h, i + 1).wait_send())
    for i in range(noise_at):
        push(i).wait_send()
    push_noise().wait_send()


def shards(white_noise, coupling, diag_inv, prior_far, prior_near, neighbours, spot_map):
    blks, subs = lax.axis_size("blk"), lax.axis_size("sub")
    owners = blks * subs
    levels, lb, draws, size = white_noise.shape
    points = spot_map.shape[0]
    per_pair = points // owners
    regroup = per_pair == LANES
    chunks = levels * lb
    secs = levels + 1
    dims = (blks, subs, levels, lb, draws, neighbours.shape[2])
    share_of = draws // subs
    half = share_of // HALVES
    out_shape = (draws, points) if regroup else (subs, chunks, share_of, size)
    dma = pltpu.SemaphoreType.DMA
    vmem = pl.BlockSpec(memory_space=pltpu.VMEM)
    hbm = pl.BlockSpec(memory_space=pltpu.HBM)
    pairs = owners if regroup else 1
    flops = 2 * draws * size * size * chunks * 7 + 4 * draws * points * points
    result = pl.pallas_call(
        functools.partial(sweep, dims, regroup),
        out_shape=jax.ShapeDtypeStruct(out_shape, BF16),
        in_specs=[hbm] * 7,
        out_specs=vmem,
        scratch_shapes=[
            pltpu.SMEM((subs, *neighbours.shape), jnp.int32),
            pltpu.VMEM((subs, *neighbours.shape), jnp.int32),
            pltpu.VMEM((subs, points // LANES, LANES), jnp.int32),
            pltpu.VMEM((subs, levels, lb, share_of, size), F32),
            pltpu.VMEM((subs, *coupling.shape), BF16),
            pltpu.VMEM((subs, *diag_inv.shape), BF16),
            [[pltpu.VMEM((owners * lb, half, size), BF16)] * HALVES] * secs,
            pltpu.VMEM((subs, chunks, share_of, size), BF16),
            pltpu.VMEM((subs, points, points), BF16),
            pltpu.VMEM((points, points), BF16),
            pltpu.VMEM((pairs, subs, share_of, LANES), BF16),
            pltpu.VMEM((pairs, draws, LANES), BF16),
            pltpu.VMEM((pairs, 8, LANES), F32),
            pltpu.VMEM((pairs, 8, LANES), F32),
            pltpu.VMEM((subs, share_of, points), F32),
            dma((levels + 4,)),
            dma((levels + 4,)),
            dma((levels + 4,)),
            dma((1,)),
            dma((2, HALVES)),
            dma((2, HALVES, blks, subs)),
            dma((2, HALVES, owners)),
            dma((levels - 1, HALVES, blks)),
            dma((levels - 1, HALVES, blks)),
            dma((owners,)),
            dma((owners,)),
            dma((owners,)),
            dma((owners,)),
            dma((1,)),
        ],
        compiler_params=pltpu.CompilerParams(
            collective_id=0, has_side_effects=True, vmem_limit_bytes=60 * 1024 * 1024),
        cost_estimate=pl.CostEstimate(flops=flops, bytes_accessed=3 * 2**20, transcendentals=0),
    )(neighbours, spot_map.reshape(points // LANES, LANES), white_noise, coupling, diag_inv,
      prior_far, prior_near)
    if regroup:
        return result
    ordering = jnp.argsort(spot_map)
    sorted_spots = jnp.take(spot_map, ordering).reshape(owners, per_pair)
    placings = lax.all_to_all(sorted_spots, OWN, split_axis=0, concat_axis=0, tiled=True)
    result = lax.all_to_all(result, "sub", split_axis=0, concat_axis=2, tiled=True)[0]
    local = result.transpose(1, 0, 2).reshape(draws, points)
    moving = jnp.take(local, ordering, axis=1).reshape(draws, owners, per_pair)
    arrived = lax.all_to_all(moving, OWN, split_axis=1, concat_axis=1, tiled=True)
    spot_local = placings.reshape(-1) % points
    return jnp.zeros((draws, points), BF16).at[:, spot_local].set(arrived.reshape(draws, points))


def solution(mesh):
    return jax.shard_map(
        shards,
        mesh=mesh,
        in_specs=(
            P(None, ("groups", "blk", "sub"), "draw", None),
            P(None, ("groups", "blk", "sub"), None, None, None),
            P(None, ("groups", "blk", "sub"), None, None),
            P(("groups", "blk", "sub"), "draw", None),
            P(("groups", "blk", "sub"), "draw", None),
            P(None, ("groups", "blk", "sub"), None),
            P(("groups", "blk", "sub")),
        ),
        out_specs=P("draw", ("groups", "blk", "sub")),
        check_vma=False,
    )
```

time: 119 us -> 34.5 us (0.29)
  blocking collectives: 71.6 us -> 0 us
  Pallas kernels: 0 us -> 32.8 us
  local copies, waits for them, and re-layouts: 18.3 us -> 1.57 us
  starting transfers between devices: 10.9 us -> 0 us
  other arithmetic: 7.13 us -> 0 us
  waiting for transfers between devices: 6.76 us -> 0 us
  matrix products: 4.01 us -> 0 us
    all_gather x5 -> x0, blocking collectives: 71.6 us -> none  [share_section(): gathered = lax.all_gather(solved, ('blk', 'sub'), axis=0, tiled=True)]
    pallas_call x0 -> x1, Pallas kernels: none -> 32.8 us  [shards(): pl.pallas_call(functools.partial(sweep, dims, regroup), out_shape=jax.Sha...]
    gather x11 -> x0, local copies, waits for them, and re-layouts: 13.1 us -> none  [the longest x8 5.18 us: lookup(): return jnp.take(gathered, neighbour_ids, axis=0)]
    all_to_all x2 -> x0, starting transfers between devices: 10.9 us -> none  [the longest x1 6.33 us: shards(): lax.all_to_all(sorted_spots, ('blk', 'sub'), split_axis=0, concat_axis=0,...]
    all_to_all x2 -> x0, waiting for transfers between devices: 6.76 us -> none  [the longest x1 6.76 us: shards(): lax.all_to_all(moving, ('blk', 'sub'), split_axis=1, concat_axis=1, tiled...]
    sort x1 -> x0, other arithmetic: 5.12 us -> none  [shards(): ordering = jnp.argsort(spot_map)]
    scatter x2 -> x0, local copies, waits for them, and re-layouts: 4.01 us -> none  [shards(): result.at[:, spot_local].set(arrived.reshape(draw_count, point_count))]
    dot_general x8 -> x0, matrix products: 4.01 us -> none  [the longest x4 2.18 us: shards(): jnp.einsum('bfp,bpq->bfq', remain, diag_inv[level_idx], preferred_element...]
  transfers between devices with their start and end apart: 2 -> 0, of which waited for: 1 -> 0; matrix products, arithmetic and copies ran while one was open for 13% -> 0% of each run, Pallas kernels for 0% -> 0%
where the time goes in v2:
time: 34.5 us; the launch traced here: 34.3 us
  Pallas kernels  32.8 us (95%)
  local copies, waits for them, and re-layouts  1.57 us (5%)
    pallas_call x1, Pallas kernels, shards(): pl.pallas_call(functools.partial(sweep, dims, regroup), out_shape=jax.Sha...  32.8 us
    unnamed x1, local copies, waits for them, and re-layouts  1.57 us

profile of v2, /device:TPU:0, one launch (start us, length us, event | category | flops | bytes accessed | tf_op | source)
XLA Modules:
  0.0 34.3 jit_solution(2296585644656688048)
XLA Ops:
  0.0 32.8 %shard_map.73 = bf16[64,1024]{1,0:T(8,128)(2,1)} custom-call(s32[4,2,6]{2,1,0:T(2,128)} %neigh_hbm.1, s32[8,128]{1,0:T(8,128)} %bitcast.1, f32[4,2,64,128]{3,2,1,0:T(8,128)} %white_hbm.1, bf16[4,2,6,128,128]{4,3,2,1,0:T(8,128)(2,1)} %coup_hbm.1, bf16[4,2,128,128]{3,2,1,0:T(8,128)(2,1)} %diag_hbm.1, bf16[2,64,128]{2,1,0:T(8,128)(2,1)} %far.1, ...), custom_call_target="tpu_custom_call" | custom-call | flops 385875968 | bytes 3145728 | tf_op jit(solution)/shard_map/pallas_call | solution.py:334
  32.8 1.6 %copy.9 = bf16[64,1024]{1,0:T(8,128)(2,1)} copy(bf16[64,1024]{1,0:T(8,128)(2,1)} %shard_map.73) | data formatting | bytes 262144

commit v3 on v2

--- a/solution.py
+++ b/solution.py
@@ -142,22 +142,22 @@
             pos_out.at[owner], pos_in.at[owner], pos_send.at[0], pos_recv.at[owner],
             device_id=device(peer(1)), device_id_type=MESH)
 
-    def landing(at, core):
-        return landed.at[pl.ds(at * subs, subs), rows_of(core), :]
-
-    def move_copy(step):
+    def landing(h, at, core):
+        return landed.at[h, pl.ds(at * subs, subs), pl.ds(pl.multiple_of(core * half, half), half), :]
+
+    def move_copy(h, step):
         to = peer(step)
         return pltpu.make_async_remote_copy(
-            moved.at[to], landing(z, c), move_send.at[step], move_recv.at[me],
+            moved.at[h, to], landing(h, z, c), move_send.at[h, step], move_recv.at[h, me],
             device_id=device(to), device_id_type=MESH)
 
-    def move_stay():
-        return pltpu.make_async_copy(moved.at[me], landing(z, c), stay_sem.at[0])
-
-    def move_arrival(at, core):
+    def move_stay(h):
+        return pltpu.make_async_copy(moved.at[h, me], landing(h, z, c), stay_sem.at[h])
+
+    def move_arrival(h, at, core):
         owner = at * subs + core
         return pltpu.make_async_remote_copy(
-            moved.at[owner], landing(at, core), move_send.at[0], move_recv.at[owner],
+            moved.at[h, owner], landing(h, at, core), move_send.at[h, 0], move_recv.at[h, owner],
             device_id=device(peer(1)), device_id_type=MESH)
 
     def lane():
@@ -236,6 +236,11 @@
         factor = coup[o, level, b, first:last].reshape((last - first) * LANES, LANES)
         return jnp.dot(rows, factor, preferred_element_type=F32)
 
+    def placed(level, o, span):
+        rows = jnp.concatenate([flat[o, level * lb + b, span, :] for b in range(lb)], axis=1)
+        width = lb * LANES
+        return jnp.dot(rows, place[o, level * width:(level + 1) * width, :], preferred_element_type=F32)
+
     blocks = [(o, b) for o in range(subs) for b in range(lb)]
     for level in range(levels):
         if level > 0:
@@ -260,45 +265,43 @@
                     pool[level + 2][h][z * (subs * lb) + o * lb + b] = solved
             if level + 1 < levels:
                 repeat(blks - 1, lambda i: level_copy(level + 2, h, i + 1).start())
-        if regroup:
+            elif regroup:
+                for o in range(subs):
+                    final = (total[o, span, :] + placed(level, o, span)).astype(BF16)
+                    for s in range(owners):
+                        moved[h, s, o] = final[:, s * LANES:(s + 1) * LANES]
+                for i in range(1, owners):
+                    move_copy(h, i).start()
+                move_stay(h).start()
+        if regroup and level + 1 < levels:
             for o in range(subs):
-                part = sum(
-                    jnp.dot(flat[o, k], place[o, k * LANES:(k + 1) * LANES, :], preferred_element_type=F32)
-                    for k in range(level * lb, (level + 1) * lb)
-                )
-                if level == 0:
-                    total[o] = part
-                elif level + 1 < levels:
-                    total[o] += part
-                else:
-                    final = (total[o] + part).astype(BF16)
-                    for s in range(owners):
-                        moved[s, o] = final[:, s * LANES:(s + 1) * LANES]
+                part = placed(level, o, slice(0, share_of))
+                total[o] = part if level == 0 else total[o] + part
             if level == 0:
                 place_arrivals()
 
     if regroup:
-        for i in range(1, owners):
-            move_copy(i).start()
-        move_stay().start()
-
-        def laid(at):
-            rows = jnp.concatenate([landed[at * subs + o] for o in range(subs)], axis=1)
+        def laid(h, at):
+            rows = jnp.concatenate([landed[h, at * subs + o] for o in range(subs)], axis=1)
             width = subs * LANES
             return jnp.dot(rows, unplace[pl.ds(pl.multiple_of(at * width, width), width), :],
                            preferred_element_type=F32)
 
-        move_stay().wait()
-        move_arrival(z, mate).wait_recv()
-        whole = laid(z)
-        for i in range(1, blks):
+        for h in range(HALVES):
+            move_stay(h).wait()
+            move_arrival(h, z, mate).wait_recv()
+            whole = laid(h, z)
+            for i in range(1, blks):
+                for core in range(subs):
+                    move_arrival(h, chip(i), core).wait_recv()
+                whole += laid(h, chip(i))
             for core in range(subs):
-                move_arrival(chip(i), core).wait_recv()
-            whole += laid(chip(i))
-        out[...] = whole.astype(BF16)
+                at = core * share_of + h * half
+                out[at:at + half, :] = whole[core * half:(core + 1) * half].astype(BF16)
         for i in range(1, owners):
             pos_copy(i).wait_send()
-            move_copy(i).wait_send()
+            for h in range(HALVES):
+                move_copy(h, i).wait_send()
     else:
         out[...] = flat[...]
     for h in range(HALVES):
@@ -333,7 +336,7 @@
     flops = 2 * draws * size * size * chunks * 7 + 4 * draws * points * points
     result = pl.pallas_call(
         functools.partial(sweep, dims, regroup),
-        out_shape=jax.ShapeDtypeStruct(out_shape, BF16),
+        out_shape=pltpu.VMEM(out_shape, BF16),
         in_specs=[hbm] * 7,
         out_specs=vmem,
         scratch_shapes=[
@@ -347,8 +350,8 @@
             pltpu.VMEM((subs, chunks, share_of, size), BF16),
             pltpu.VMEM((subs, points, points), BF16),
             pltpu.VMEM((points, points), BF16),
-            pltpu.VMEM((pairs, subs, share_of, LANES), BF16),
-            pltpu.VMEM((pairs, draws, LANES), BF16),
+            pltpu.VMEM((HALVES, pairs, subs, half, LANES), BF16),
+            pltpu.VMEM((HALVES, pairs, subs * half, LANES), BF16),
             pltpu.VMEM((pairs, 8, LANES), F32),
             pltpu.VMEM((pairs, 8, LANES), F32),
             pltpu.VMEM((subs, share_of, points), F32),
@@ -363,9 +366,9 @@
             dma((levels - 1, HALVES, blks)),
             dma((owners,)),
             dma((owners,)),
-            dma((owners,)),
-            dma((owners,)),
-            dma((1,)),
+            dma((HALVES, owners)),
+            dma((HALVES, owners)),
+            dma((HALVES,)),
         ],
         compiler_params=pltpu.CompilerParams(
             collective_id=0, has_side_effects=True, vmem_limit_bytes=60 * 1024 * 1024),

time: 34.5 us -> 33.1 us (0.959)
  local copies, waits for them, and re-layouts: 1.57 us -> 0.66 us
  Pallas kernels: 32.8 us -> 32.2 us
    unnamed x1, local copies, waits for them, and re-layouts: 1.57 us -> 0.66 us
    pallas_call x1, Pallas kernels: 32.8 us -> 32.2 us  [shards(): pl.pallas_call(functools.partial(sweep, dims, regroup), out_shape=pltpu.V...]
where the time goes in v3:
time: 33.1 us; the launch traced here: 32.9 us
  Pallas kernels  32.2 us (97%)
  local copies, waits for them, and re-layouts  0.66 us (2%)
    pallas_call x1, Pallas kernels, shards(): pl.pallas_call(functools.partial(sweep, dims, regroup), out_shape=pltpu.V...  32.2 us

profile of v3, /device:TPU:0, one launch (start us, length us, event | category | flops | bytes accessed | tf_op | source)
XLA Modules:
  0.0 32.9 jit_solution(12395483662278391627)
XLA Ops:
  0.0 32.2 %shard_map.73 = bf16[64,1024]{1,0:T(8,128)(2,1)S(1)} custom-call(s32[4,2,6]{2,1,0:T(2,128)} %neigh_hbm.1, s32[8,128]{1,0:T(8,128)} %bitcast.1, f32[4,2,64,128]{3,2,1,0:T(8,128)} %white_hbm.1, bf16[4,2,6,128,128]{4,3,2,1,0:T(8,128)(2,1)} %coup_hbm.1, bf16[4,2,128,128]{3,2,1,0:T(8,128)(2,1)} %diag_hbm.1, bf16[2,64,128]{2,1,0:T(8,128)(2,1)} %far.1, ...), custom_call_target="tpu_custom_call" | custom-call | flops 385875968 | bytes 3145728 | tf_op jit(solution)/shard_map/pallas_call | solution.py:337
  32.2 0.7 %copy.9 = bf16[64,1024]{1,0:T(8,128)(2,1)} copy(bf16[64,1024]{1,0:T(8,128)(2,1)S(1)} %shard_map.73) | data formatting | bytes 262144

commit v4 on v3

--- a/solution.py
+++ b/solution.py
@@ -202,9 +202,6 @@
     for i in range(2, noise_at):
         load(i).start()
     load_noise().start()
-    load(0).wait()
-    if regroup:
-        rank_points(c, True)
     pl.semaphore_wait(barrier, owners - 1)
     for sec in (1, 0):
         share_prior(sec, 0)
@@ -216,12 +213,12 @@
             share_prior(sec, h)
     for i in range(4, noise_at):
         push(i).start()
+    load(0).wait()
     if regroup:
+        rank_points(c, True)
         for i in range(1, owners):
             pos_copy(i).start()
     push(0).wait_recv()
-    if regroup:
-        rank_points(mate, False)
     ready(1)
     to_smem = pltpu.make_async_copy(neigh_vm, neigh, smem_sem.at[0])
     to_smem.start()
@@ -273,11 +270,13 @@
                 for i in range(1, owners):
                     move_copy(h, i).start()
                 move_stay(h).start()
+        if regroup and level == 0:
+            rank_points(mate, False)
         if regroup and level + 1 < levels:
             for o in range(subs):
                 part = placed(level, o, slice(0, share_of))
                 total[o] = part if level == 0 else total[o] + part
-            if level == 0:
+            if level == 1:
                 place_arrivals()
 
     if regroup:

time: 33.1 us -> 32.5 us (0.982)
  Pallas kernels: 32.2 us -> 31.6 us
    pallas_call x1, Pallas kernels: 32.2 us -> 31.6 us  [shards(): pl.pallas_call(functools.partial(sweep, dims, regroup), out_shape=pltpu.V...]
where the time goes in v4:
time: 32.5 us; the launch traced here: 32.3 us
  Pallas kernels  31.6 us (97%)
  local copies, waits for them, and re-layouts  0.66 us (2%)
    pallas_call x1, Pallas kernels, shards(): pl.pallas_call(functools.partial(sweep, dims, regroup), out_shape=pltpu.V...  31.6 us
    unnamed x1, local copies, waits for them, and re-layouts  0.66 us

profile of v4, /device:TPU:0, one launch (start us, length us, event | category | flops | bytes accessed | tf_op | source)
XLA Modules:
  0.0 32.3 jit_solution(13137388451216676831)
XLA Ops:
  0.0 31.6 %shard_map.73 = bf16[64,1024]{1,0:T(8,128)(2,1)S(1)} custom-call(s32[4,2,6]{2,1,0:T(2,128)} %neigh_hbm.1, s32[8,128]{1,0:T(8,128)} %bitcast.1, f32[4,2,64,128]{3,2,1,0:T(8,128)} %white_hbm.1, bf16[4,2,6,128,128]{4,3,2,1,0:T(8,128)(2,1)} %coup_hbm.1, bf16[4,2,128,128]{3,2,1,0:T(8,128)(2,1)} %diag_hbm.1, bf16[2,64,128]{2,1,0:T(8,128)(2,1)} %far.1, ...), custom_call_target="tpu_custom_call" | custom-call | flops 385875968 | bytes 3145728 | tf_op jit(solution)/shard_map/pallas_call | solution.py:336
  31.7 0.7 %copy.9 = bf16[64,1024]{1,0:T(8,128)(2,1)} copy(bf16[64,1024]{1,0:T(8,128)(2,1)S(1)} %shard_map.73) | data formatting | bytes 262144
